TPU v7x, 32 devices: a whole 2x2x4 slice. The times are simulated.
32 devices in a mesh: groups: 2 (over x), brick: 4 (over y, core), tm: 4 (over z).
Axes of the slice: x: 2, y: 2, z: 4, core: 2. Of those that a mesh axis runs over, the one named last changes fastest.
Arguments:
- link_rows: float32 [8, 2, 2, 3, 8, 8, 768], P('groups', None, None, None, 'brick', 'tm'), parts along dimension 0, may hold values from -1 to 1, as said below
- target: float32 [8, 8, 8, 8, 768], P('groups', None, 'brick', 'tm'), parts along dimension 0, may hold values from -6 to 6
- weights: float32 [4, 6], replicated, may hold values from -3 to 3
Outputs:
- weight_grad: float32 [8, 6], P('groups'), parts along dimension 0
- link_force: float32 [8, 8, 8, 8, 768], P('groups', None, 'brick', 'tm'), parts along dimension 0
There are 2 independent parts, one for each index of `groups`. A program takes and returns all parts, laid end to end along the dimension named above; an argument that names none is the same for every part. Nothing has to cross between parts.
Inputs may be any that keep to these rules, and one draw needn't show every extreme that they name: `link_rows`: the two rows of each link are orthonormal complex vectors, so every rebuilt link is special unitary.
All inputs are finite; a program needn't handle non-finite values.
Results may differ from a plain program's by a relative error of at most 0.0003.
Values sent between devices are 32-bit elements; how exact they have to be, the bound alone decides.
A program may use at most 256 MiB of HBM per device.

v0:
```python
import jax
import jax.numpy as jnp
from jax import lax
from jax.experimental import pallas as pl
from jax.experimental.pallas import tpu as pltpu
from jax.sharding import PartitionSpec as P

NZ = 16
LANES = 128
ROOT_THREE = 3.0**0.5
VMEM = pl.BlockSpec(memory_space=pltpu.VMEM)
SMEM = pl.BlockSpec(memory_space=pltpu.SMEM)


def mul(a, b):
    return a[0] * b[0] - a[1] * b[1], a[0] * b[1] + a[1] * b[0]


def mul_conj(a, b):
    return a[0] * b[0] + a[1] * b[1], a[1] * b[0] - a[0] * b[1]


def add(*terms):
    re, im = terms[0]
    for t in terms[1:]:
        re, im = re + t[0], im + t[1]
    return re, im


def sub(a, b):
    return a[0] - b[0], a[1] - b[1]


def conj(a):
    return a[0], -a[1]


def scale(a, s):
    return a[0] * s, a[1] * s


def cross_row(r, s):
    out = []
    for i, j in ((1, 2), (2, 0), (0, 1)):
        out.append(conj(sub(mul(r[i], s[j]), mul(r[j], s[i]))))
    return out


def product(a, b):
    rows = [
        [add(mul(a[i][0], b[0][k]), mul(a[i][1], b[1][k]), mul(a[i][2], b[2][k])) for k in range(3)]
        for i in range(2)
    ]
    return rows + [cross_row(*rows)]


def product_dagger(a, b):
    rows = [
        [
            add(mul_conj(a[i][0], b[k][0]), mul_conj(a[i][1], b[k][1]), mul_conj(a[i][2], b[k][2]))
            for k in range(3)
        ]
        for i in range(2)
    ]
    return rows + [cross_row(*rows)]


def dagger(a):
    return [[conj(a[j][i]) for j in range(3)] for i in range(3)]


def conjugated(u, h):
    d0, d1, h01, h02, h12 = h
    t = []
    for i in range(2):
        a, b, c = u[i]
        t.append(
            [
                add(scale(a, d0), mul_conj(b, h01), mul_conj(c, h02)),
                add(scale(b, d1), mul(a, h01), mul_conj(c, h12)),
                add(mul(a, h02), mul(b, h12)),
            ]
        )

    def entry(i, j):
        return add(*[mul_conj(t[i][k], u[j][k]) for k in range(3)])

    def diagonal(i):
        return sum(t[i][k][0] * u[i][k][0] + t[i][k][1] * u[i][k][1] for k in range(3))

    e0, e1 = diagonal(0), diagonal(1)
    e2 = d0 + d1 - e0 - e1
    return e0 - e2, e1 - e2, entry(0, 1), entry(0, 2), entry(1, 2)


def flat(h):
    d0, d1, a, b, c = h
    return [d0, d1, *a, *b, *c]


def unflat(v):
    return v[0], v[1], (v[2], v[3]), (v[4], v[5]), (v[6], v[7])


def hermitian_part(p):
    return (
        [p[k][k][0] for k in range(3)],
        *[
            (0.5 * (p[i][j][0] + p[j][i][0]), 0.5 * (p[i][j][1] - p[j][i][1]))
            for i, j in ((0, 1), (0, 2), (1, 2))
        ],
    )


def anti_part(p):
    d = [p[k][k][1] for k in range(3)]
    return (
        d[0] - d[2],
        d[1] - d[2],
        *[
            (0.5 * (p[i][j][1] + p[j][i][1]), 0.5 * (p[j][i][0] - p[i][j][0]))
            for i, j in ((0, 1), (0, 2), (1, 2))
        ],
    )


def half_anticommutator(pr, q):
    p, p01, p02, p12 = pr
    d0, d1, q01, q02, q12 = q
    mean = (d0 + d1) * (1.0 / 3.0)
    q0, q1, q2 = d0 - mean, d1 - mean, -mean
    e01 = add(scale(q01, p[0] + p[1]), scale(p01, -q2), mul_conj(p02, q12), mul_conj(q02, p12))
    e02 = add(scale(q02, p[0] + p[2]), scale(p02, -q1), mul(p01, q12), mul(q01, p12))
    e12 = add(scale(q12, p[1] + p[2]), scale(p12, -q0), mul_conj(q02, p01), mul_conj(p02, q01))
    x01 = p01[0] * q01[0] + p01[1] * q01[1]
    x02 = p02[0] * q02[0] + p02[1] * q02[1]
    x12 = p12[0] * q12[0] + p12[1] * q12[1]
    last = p[2] * q2
    return (
        p[0] * q0 - last + x01 - x12,
        p[1] * q1 - last + x01 - x02,
        scale(e01, 0.5),
        scale(e02, 0.5),
        scale(e12, 0.5),
    )


def i_commutator(x, y):
    x0, x1, x01, x02, x12 = x
    y0, y1, y01, y02, y12 = y
    c01 = sub(add(scale(y01, x0 - x1), scale(x01, y1 - y0), mul_conj(x02, y12)), mul_conj(y02, x12))
    c02 = sub(add(scale(y02, x0), scale(x02, -y0), mul(x01, y12)), mul(y01, x12))
    c12 = sub(add(scale(y12, x1), scale(x12, -y1), mul_conj(y02, x01)), mul_conj(x02, y01))
    a01 = x01[1] * y01[0] - x01[0] * y01[1]
    a02 = x02[1] * y02[0] - x02[0] * y02[1]
    a12 = x12[1] * y12[0] - x12[0] * y12[1]
    d2 = 2.0 * (a02 + a12)
    return (
        -2.0 * (a01 + a02) - d2,
        2.0 * (a01 - a12) - d2,
        (-c01[1], c01[0]),
        (-c02[1], c02[0]),
        (-c12[1], c12[0]),
    )


def plane(p):
    mu = jnp.where(p < 3, 0, jnp.where(p < 5, 1, 2))
    nu = jnp.where(p < 3, p + 1, jnp.where(p < 5, p - 1, 3))
    return mu, nu


PLANES = ((0, 1), (0, 2), (0, 3), (1, 2), (1, 3), (2, 3))


def grid_of(shape):
    lane = lax.broadcasted_iota(jnp.int32, shape, 1)
    row = lax.broadcasted_iota(jnp.int32, shape, 0)
    return row, lane


def move_z(v, step):
    row, lane = grid_of(v.shape)
    inside = pltpu.roll(v, (-step) % LANES, 1)
    across = pltpu.roll(v, (step * (NZ - 1)) % LANES, 1)
    edge = NZ - 1 if step > 0 else 0
    return jnp.where(lane % NZ == edge, across, inside)


def move_y(v, step, per_cell):
    rows = v.shape[0]
    row, lane = grid_of(v.shape)
    turned = pltpu.roll(v, (-step * NZ) % LANES, 1)
    inside = pltpu.roll(turned, (-step) % rows, 0)
    across = pltpu.roll(turned, (step * (per_cell - 1)) % rows, 0)
    edge = per_cell - 1 if step > 0 else 0
    other = jnp.where(row % per_cell == edge, across, inside)
    over = lane >= LANES - NZ if step > 0 else lane < NZ
    return jnp.where(over, other, turned)


def load_matrix(ref, index, rows):
    at = lambda c: ref[(*index, c, rows, slice(None))]
    return [[(at(3 * i + j), at(9 + 3 * i + j)) for j in range(3)] for i in range(3)]


def store_matrix(ref, index, rows, m):
    for i in range(3):
        for j in range(3):
            for part in range(2):
                ref[(*index, 9 * part + 3 * i + j, rows, slice(None))] = m[i][j][part]


def load_flat(ref, index, rows):
    return unflat([ref[(*index, c, rows, slice(None))] for c in range(8)])


def store_flat(ref, index, rows, h):
    for c, v in enumerate(flat(h)):
        ref[(*index, c, rows, slice(None))] = v


def add_flat(ref, index, rows, h):
    for c, v in enumerate(flat(h)):
        ref[(*index, c, rows, slice(None))] += v


def complete_into(src, src_index, dst, dst_index, total):
    def chunk(k, carry):
        rows = pl.ds(pl.multiple_of(8 * k, 8), 8)
        at = lambda c: src[(*src_index, c, rows, slice(None))]
        m = [[(at(3 * i + j), at(6 + 3 * i + j)) for j in range(3)] for i in range(2)]
        m.append(cross_row(*m))
        store_matrix(dst, dst_index, rows, m)
        return carry

    lax.fori_loop(0, total // 8, chunk, 0)


def loops_kernel(per_cell, own, along_x, along_t, plaq, here, moved_b, moved_c, full):
    total = own.shape[2]
    for d in range(4):
        complete_into(own, (d,), full, (0, d), total)
    for k in range(3):
        complete_into(along_x, (k,), full, (1, k + 1), total)
        complete_into(along_t, (k,), full, (4, k), total)

    def shift_links(c, carry):
        for d in range(4):
            value = full[0, d, c]
            if d != 1:
                full[2, d, c] = move_y(value, 1, per_cell)
            if d != 2:
                full[3, d, c] = move_z(value, 1)
        return carry

    lax.fori_loop(0, 18, shift_links, 0)
    chunks = total // 8

    def step(i, carry):
        p = i // chunks
        rows = pl.ds(pl.multiple_of(8 * (i % chunks), 8), 8)
        mu, nu = plane(p)
        a = load_matrix(full, (0, mu), rows)
        b = load_matrix(full, (1 + mu, nu), rows)
        c = load_matrix(full, (1 + nu, mu), rows)
        d = load_matrix(full, (0, nu), rows)
        loop = product_dagger(product(a, b), product(d, c))
        store_matrix(plaq, (p,), rows, loop)
        pi = anti_part(loop)
        store_flat(here, (p,), rows, pi)
        store_flat(moved_b, (p,), rows, conjugated(dagger(a), pi))
        store_flat(moved_c, (p,), rows, conjugated(dagger(d), pi))
        return carry

    lax.fori_loop(0, 6 * chunks, step, 0)

    def shift_back(c, carry):
        for p in (3, 4):
            moved_b[p, c] = move_y(moved_b[p, c], -1, per_cell)
        moved_b[5, c] = move_z(moved_b[5, c], -1)
        moved_c[0, c] = move_y(moved_c[0, c], -1, per_cell)
        for p in (1, 3):
            moved_c[p, c] = move_z(moved_c[p, c], -1)
        return carry

    lax.fori_loop(0, 8, shift_back, 0)


def residual_kernel(weights, target, here, moved_b, moved_c, from_x, from_t, residual, sums):
    total = target.shape[2]

    def chunk(k, carry):
        rows = pl.ds(pl.multiple_of(8 * k, 8), 8)
        acc = []
        for mu in range(4):
            terms = []
            for j in range(3):
                nu = [n for n in range(4) if n != mu][j]
                p = PLANES.index((min(mu, nu), max(mu, nu)))
                load = lambda ref, index: [ref[index, c, rows, :] for c in range(8)]
                if mu < nu:
                    sign = 1.0
                    up = load(here, p)
                    low = load(from_t, (2, 4, 5).index(p)) if nu == 3 else load(moved_c, p)
                else:
                    sign = -1.0
                    up = load(here, p)
                    low = load(from_x, p) if nu == 0 else load(moved_b, p)
                terms.append((sign, up))
                terms.append((-sign, low))
            v = [
                sum(terms[s][1][c] * (terms[s][0] * weights[mu, s]) for s in range(6))
                for c in range(8)
            ]
            t = [target[mu, a, rows, :] for a in range(8)]
            r3 = v[0] - v[1] - t[2]
            r8 = (v[0] + v[1]) * (1.0 / ROOT_THREE) - t[7]
            r = [
                r3 + ROOT_THREE * r8,
                ROOT_THREE * r8 - r3,
                2.0 * v[2] - t[0],
                2.0 * v[3] + t[1],
                2.0 * v[4] - t[3],
                2.0 * v[5] + t[4],
                2.0 * v[6] - t[5],
                2.0 * v[7] + t[6],
            ]
            for c in range(8):
                residual[mu, c, rows, :] = r[c]
            g = [r3 + r8 * (1.0 / ROOT_THREE), r8 * (1.0 / ROOT_THREE) - r3]
            g += [2.0 * x for x in r[2:]]
            for sign, w in terms:
                acc.append(sign * sum(g[c] * w[c] for c in range(8)))
        return tuple(x + y for x, y in zip(carry, acc))

    zero = jnp.zeros((8, LANES), jnp.float32)
    acc = lax.fori_loop(0, total // 8, chunk, (zero,) * 24)
    for n, x in enumerate(acc):
        sums[n : n + 1, :] = jnp.sum(x, axis=0, keepdims=True)


def force_kernel(
    per_cell, weights, own, plaq, residual, along_x, along_t, force, to_x, to_t, full, res, back_b, back_c
):
    total = own.shape[2]
    for d in range(4):
        complete_into(own, (d,), full, (d,), total)

    def shift_residual(c, carry):
        for d in range(4):
            value = residual[d, c]
            res[0, d, c] = value
            if d != 1:
                res[2, d, c] = move_y(value, 1, per_cell)
            if d != 2:
                res[3, d, c] = move_z(value, 1)
            force[d, c] = jnp.zeros_like(value)
        for k in range(3):
            res[1, k + 1, c] = along_x[k, c]
            res[4, k, c] = along_t[k, c]
        return carry

    lax.fori_loop(0, 8, shift_residual, 0)
    chunks = total // 8

    def step(i, carry):
        p = i // chunks
        rows = pl.ds(pl.multiple_of(8 * (i % chunks), 8), 8)
        mu, nu = plane(p)
        wa, wc = weights[mu, 2 * (nu - 1)], weights[mu, 2 * (nu - 1) + 1]
        wd, wb = weights[nu, 2 * mu], weights[nu, 2 * mu + 1]
        a = load_matrix(full, (mu,), rows)
        d = load_matrix(full, (nu,), rows)
        loop = load_matrix(plaq, (p,), rows)
        pr, pi = hermitian_part(loop), anti_part(loop)
        sb = [x * wb for x in flat(conjugated(a, load_flat(res, (1 + mu, nu), rows)))]
        sc = [x * wc for x in flat(conjugated(d, load_flat(res, (1 + nu, mu), rows)))]
        ra = flat(load_flat(res, (0, mu), rows))
        rd = flat(load_flat(res, (0, nu), rows))
        q = unflat([wa * ra[c] - wd * rd[c] + sb[c] - sc[c] for c in range(8)])
        e = flat(half_anticommutator(pr, q))
        k = [0.5 * x for x in flat(i_commutator(pi, q))]
        fore = [x + y for x, y in zip(e, k)]
        aft = [y - x for x, y in zip(e, k)]
        store_flat(back_b, (p,), rows, conjugated(dagger(a), unflat(fore)))
        store_flat(back_c, (p,), rows, conjugated(dagger(d), unflat(aft)))
        xb = flat(i_commutator(pi, unflat(sb)))
        xc = flat(i_commutator(pi, unflat(sc)))
        add_flat(force, (mu,), rows, unflat([x - y for x, y in zip(fore, xb)]))
        add_flat(force, (nu,), rows, unflat([x + y for x, y in zip(aft, xc)]))
        return carry

    lax.fori_loop(0, 6 * chunks, step, 0)

    def shift_back(c, carry):
        for k in range(3):
            to_x[k, c] = back_b[k, c]
            to_t[k, c] = back_c[(2, 4, 5)[k], c]
        force[2, c] += move_y(back_b[3, c], -1, per_cell)
        force[3, c] += move_y(back_b[4, c], -1, per_cell) + move_z(back_b[5, c], -1)
        force[0, c] += move_y(back_c[0, c], -1, per_cell) + move_z(back_c[1, c], -1)
        force[1, c] += move_z(back_c[3, c], -1)
        return carry

    lax.fori_loop(0, 8, shift_back, 0)


def body(link_rows, target, weights):
    f32 = jnp.float32
    nx, nt, plane_sites = link_rows.shape[4:]
    bricks, tms = lax.axis_size("brick"), lax.axis_size("tm")
    sites = nx * nt * plane_sites
    total = sites // LANES
    per_cell = plane_sites // LANES
    size = lambda *lead: jax.ShapeDtypeStruct((*lead, total, LANES), f32)
    params = pltpu.CompilerParams(vmem_limit_bytes=48 * 1024 * 1024)

    def ahead(values, axis, dim):
        dim = values.ndim - dim
        n = lax.axis_size(axis)
        first = lax.slice_in_dim(values, 0, 1, axis=dim)
        rest = lax.slice_in_dim(values, 1, values.shape[dim], axis=dim)
        first = lax.ppermute(first, axis, [((i + 1) % n, i) for i in range(n)])
        return jnp.concatenate([rest, first], axis=dim)

    def behind(values, axis, dim):
        dim = values.ndim - dim
        n = lax.axis_size(axis)
        extent = values.shape[dim]
        last = lax.slice_in_dim(values, extent - 1, extent, axis=dim)
        rest = lax.slice_in_dim(values, 0, extent - 1, axis=dim)
        last = lax.ppermute(last, axis, [(i, (i + 1) % n) for i in range(n)])
        return jnp.concatenate([last, rest], axis=dim)

    def spread(values):
        return values.reshape(*values.shape[:-2], nx, nt, plane_sites)

    def packed(values, count):
        return values.reshape(-1, count, total, LANES)

    own = packed(link_rows, 12)
    links_x = packed(ahead(link_rows[1:4], "brick", 3), 12)
    links_t = packed(ahead(link_rows[0:3], "tm", 2), 12)
    plaq, here, moved_b, moved_c = pl.pallas_call(
        lambda *refs: loops_kernel(per_cell, *refs),
        out_shape=(size(6, 18), size(6, 8), size(6, 8), size(6, 8)),
        in_specs=[VMEM] * 3,
        out_specs=(VMEM,) * 4,
        scratch_shapes=[pltpu.VMEM((5, 4, 18, total, LANES), f32)],
        compiler_params=params,
        name="loops",
    )(own, links_x, links_t)
    from_x = packed(behind(spread(moved_b[0:3]), "brick", 3), 8)
    from_t = packed(
        behind(spread(jnp.stack([moved_c[2], moved_c[4], moved_c[5]])), "tm", 2), 8
    )
    residual, sums = pl.pallas_call(
        residual_kernel,
        out_shape=(size(4, 8), jax.ShapeDtypeStruct((24, LANES), f32)),
        in_specs=[SMEM] + [VMEM] * 6,
        out_specs=(VMEM, VMEM),
        compiler_params=params,
        name="residual",
    )(weights, packed(target, 8), here, moved_b, moved_c, from_x, from_t)
    weight_grad = lax.psum(jnp.sum(sums, axis=1).reshape(4, 6), ("brick", "tm"))
    weight_grad = weight_grad / (sites * bricks * tms)
    res_x = packed(ahead(spread(residual[1:4]), "brick", 3), 8)
    res_t = packed(ahead(spread(residual[0:3]), "tm", 2), 8)
    force, to_x, to_t = pl.pallas_call(
        lambda *refs: force_kernel(per_cell, *refs),
        out_shape=(size(4, 8), size(3, 8), size(3, 8)),
        in_specs=[SMEM] + [VMEM] * 5,
        out_specs=(VMEM,) * 3,
        scratch_shapes=[
            pltpu.VMEM((4, 18, total, LANES), f32),
            pltpu.VMEM((5, 4, 8, total, LANES), f32),
            pltpu.VMEM((6, 8, total, LANES), f32),
            pltpu.VMEM((6, 8, total, LANES), f32),
        ],
        compiler_params=params,
        name="force",
    )(weights, own, plaq, residual, res_x, res_t)
    f = spread(force)
    fx = behind(spread(to_x), "brick", 3)
    ft = behind(spread(to_t), "tm", 2)
    zero = jnp.zeros_like(fx[:1])
    h = f + jnp.concatenate([zero, fx]) + jnp.concatenate([ft, zero])
    link_force = jnp.stack(
        [
            2.0 * h[:, 2],
            -2.0 * h[:, 3],
            h[:, 0] - h[:, 1],
            2.0 * h[:, 4],
            -2.0 * h[:, 5],
            2.0 * h[:, 6],
            -2.0 * h[:, 7],
            (h[:, 0] + h[:, 1]) * (1.0 / ROOT_THREE),
        ],
        axis=1,
    )
    return weight_grad, link_force


def solution(mesh):
    in_specs = (
        P("groups", None, None, None, "brick", "tm", None),
        P("groups", None, "brick", "tm", None),
        P(),
    )
    out_specs = (P("groups", None), P("groups", None, "brick", "tm", None))
    return jax.shard_map(body, mesh=mesh, in_specs=in_specs, out_specs=out_specs, check_vma=False)
```

profile of v0, /device:TPU:0, one launch (start us, length us, event | category | flops | bytes accessed | tf_op | source)
XLA Modules:
  0.0 96.4 jit_solution(8681011599999383710)
XLA Ops:
  0.6 1.1 %fusion.9 = (f32[3,2,2,3,1,2,768]{6,5,4,3,2,1,0:T(2,128)S(1)}, f32[3,2,2,3,1,2,768]{6,5,4,3,2,1,0:T(2,128)S(1)}) fusion(f32[4,2,2,3,2,2,768]{6,5,4,3,2,1,0:T(2,128)} %param.3), kind=kLoop, calls=%fused_computation.27 | loop fusion | bytes 884736 | tf_op jit(solution)/shard_map/slice | solution.py:423
  1.8 2.5 %collective-permute-start = (f32[3,2,2,3,1,2,768]{6,5,4,3,2,1,0:T(2,128)S(1)}, f32[3,2,2,3,1,2,768]{6,5,4,3,2,1,0:T(2,128)S(1)}, u32[]{:S(2)}, u32[]{:S(2)}) collective-permute-start(f32[3,2,2,3,1,2,768]{6,5,4,3,2,1,0:T(2,128)S(1)} %get-tuple-element.23), channel_id=1, source_target_pairs={{4,0},{8,4},{12,8},{0,12},{5,1},{9,5},{13,9},{1,13},{6,2},{10,6},{... | collective-permute-start | bytes 663560 | tf_op jit(solution)/shard_map/ppermute | solution.py:424
  4.3 1.5 %fusion.8 = (f32[3,2,2,3,2,1,768]{6,5,4,3,2,1,0:T(1,128)S(1)}, f32[3,2,2,3,2,1,768]{6,5,4,3,2,1,0:T(1,128)S(1)}) fusion(f32[4,2,2,3,2,2,768]{6,5,4,3,2,1,0:T(2,128)} %param.3), kind=kLoop, calls=%fused_computation.26 | loop fusion | bytes 884736 | tf_op jit(solution)/shard_map/slice | solution.py:423
  5.8 3.7 %collective-permute-start.1 = (f32[3,2,2,3,2,1,768]{6,5,4,3,2,1,0:T(1,128)S(1)}, f32[3,2,2,3,2,1,768]{6,5,4,3,2,1,0:T(1,128)S(1)}, u32[]{:S(2)}, u32[]{:S(2)}) collective-permute-start(f32[3,2,2,3,2,1,768]{6,5,4,3,2,1,0:T(1,128)S(1)} %get-tuple-element.21), channel_id=1, source_target_pairs={{1,0},{2,1},{3,2},{0,3},{5,4},{6,5},{7,6},{4,7},{9,8},{10,9},{11,1... | collective-permute-start | bytes 663560 | tf_op jit(solution)/shard_map/ppermute | solution.py:424
  9.5 0.5 reshape.53.refs_0_.refs_1_
  9.9 0.2 pad_maximum_fusion
  10.1 0.4 reshape.54.refs_1_
  10.5 3.4 %collective-permute-done.1 = f32[3,2,2,3,2,1,768]{6,5,4,3,2,1,0:T(1,128)S(1)} collective-permute-done((f32[3,2,2,3,2,1,768]{6,5,4,3,2,1,0:T(1,128)S(1)}, f32[3,2,2,3,2,1,768]{6,5,4,3,2,1,0:T(1,128)S(1)}, u32[]{:S(2)}, u32[]{:S(2)}) %collective-permute-start.1) | collective-permute-done | bytes 221216 | tf_op jit(solution)/shard_map/ppermute | solution.py:424
  13.9 0.4 pad_maximum_fusion.1
  14.3 0.4 reshape.55.refs_2_
  14.6 5.5 %loops.1 = (f32[6,18,24,128]{3,2,1,0:T(8,128)S(1)}, f32[6,8,24,128]{3,2,1,0:T(8,128)S(1)}, f32[6,8,24,128]{3,2,1,0:T(8,128)S(1)}, f32[6,8,24,128]{3,2,1,0:T(8,128)S(1)}) custom-call(f32[4,12,24,128]{3,2,1,0:T(8,128)S(1)} %reshape.53.refs_0_.refs_1_, f32[3,12,24,128]{3,2,1,0:T(8,128)S(1)} %reshape.54.refs_1_, f32[3,12,24,128]{3,2,1,0:T(8,128)S(1)} %reshape.55.refs_2_), custom_call_target="tpu_custom_call" | custom-call | tf_op jit(solution)/shard_map/loops/pallas_call | solution.py:445
  20.2 0.8 copy-done.4
  21.0 0.8 copy-done
  21.8 0.2 reshape.58
  22.0 0.9 fusion.15
  22.9 0.5 collective-permute-start.3
  23.5 0.7 fusion.16
  24.3 1.3 %reshape.52.target = f32[4,8,24,128]{3,2,1,0:T(8,128)S(1)} reshape(f32[4,8,2,2,768]{4,3,2,1,0:T(2,128)} %param.4) | data formatting | bytes 786432 | tf_op jit(solution)/shard_map/reshape | solution.py:440
  25.6 5.0 %collective-permute-done.3 = f32[3,8,2,1,768]{4,3,2,1,0:T(1,128)} collective-permute-done((f32[3,8,2,1,768]{4,3,2,1,0:T(1,128)}, f32[3,8,2,1,768]{4,3,2,1,0:T(1,128)}, u32[]{:S(2)}, u32[]{:S(2)}) %collective-permute-start.3) | collective-permute-done | bytes 147488 | tf_op jit(solution)/shard_map/ppermute | solution.py:433
  30.6 1.2 %pad_maximum_fusion.4 = f32[3,8,2,2,768]{4,3,2,1,0:T(2,128)S(1)} fusion(f32[3,8,2,1,768]{4,3,2,1,0:T(1,128)S(1)} %get-tuple-element.35, f32[3,8,2,1,768]{4,3,2,1,0:T(1,128)} %collective-permute-done.3), kind=kLoop, calls=%fused_computation.8 | loop fusion | flops 73728 | bytes 589824 | tf_op jit(solution)/shard_map/concatenate | solution.py:434
  31.8 0.9 reshape.59.from_t
  32.7 1.1 %pad_maximum_fusion.2 = f32[3,8,2,2,768]{4,3,2,1,0:T(2,128)S(1)} fusion(f32[3,8,1,2,768]{4,3,2,1,0:T(2,128)} %get-tuple-element.37, f32[3,8,1,2,768]{4,3,2,1,0:T(2,128)} %collective-permute-done.2), kind=kLoop, calls=%fused_computation.6 | loop fusion | flops 73728 | bytes 589824 | tf_op jit(solution)/shard_map/concatenate | solution.py:434
  33.8 1.0 reshape.57.from_x
  34.8 1.1 %copy-done.1 = f32[6,8,24,128]{3,2,1,0:T(8,128)S(1)} copy-done((f32[6,8,24,128]{3,2,1,0:T(8,128)S(1)}, f32[6,8,24,128]{3,2,1,0:T(8,128)}, u32[]{:S(2)}) %copy-start.1) | copy-done | bytes 589848
  35.9 1.0 copy-done.2
  36.8 1.0 copy-done.3
  37.8 1.1 %copy-done.5 = f32[6,8,24,128]{3,2,1,0:T(8,128)S(1)} copy-done((f32[6,8,24,128]{3,2,1,0:T(8,128)S(1)}, f32[6,8,24,128]{3,2,1,0:T(8,128)}, u32[]{:S(2)}) %copy-start.5) | copy-done | bytes 589848
  38.9 1.0 %residual.1 = (f32[4,8,24,128]{3,2,1,0:T(8,128)S(1)}, f32[24,128]{1,0:T(8,128)S(1)}) custom-call(f32[4,6]{1,0:T(4,128)S(1)} %copy-done.9, f32[4,8,24,128]{3,2,1,0:T(8,128)S(1)} %reshape.52.target, f32[6,8,24,128]{3,2,1,0:T(8,128)S(1)} %copy-done.5, f32[6,8,24,128]{3,2,1,0:T(8,128)S(1)} %get-tuple-element.12.moved_b, f32[6,8,24,128]{3,2,1,0:T(8,128)S(1)} %copy-done.1, ...), custom_call_target="tpu_custom_call" | custom-call | tf_op jit(solution)/shard_map/residual/pallas_call | solution.py:458
  40.1 0.2 fusion.13
  40.3 2.1 %collective-permute-start.5 = (f32[3,8,2,1,768]{4,3,2,1,0:T(1,128)S(1)}, f32[3,8,2,1,768]{4,3,2,1,0:T(1,128)}, u32[]{:S(2)}, u32[]{:S(2)}) collective-permute-start(f32[3,8,2,1,768]{4,3,2,1,0:T(1,128)S(1)} %get-tuple-element.31), channel_id=1, source_target_pairs={{1,0},{2,1},{3,2},{0,3},{5,4},{6,5},{7,6},{4,7},{9,8},{10,9},{11,1... | collective-permute-start | bytes 442376 | tf_op jit(solution)/shard_map/ppermute | solution.py:424
  42.6 0.7 fusion.14
  43.5 31.0 %psum.7 = f32[4,6]{1,0:T(4,128)S(1)} all-reduce(f32[4,6]{1,0:T(4,128)S(1)} %reshape.60), channel_id=1, replica_groups=mesh['groups'=2,'brick'=4,'tm'=4] {'brick','tm'}, use_global_device_ids=true, to_apply=%region_1.0 | all-reduce | flops 24 | bytes 192 | tf_op jit(solution)/shard_map/psum | solution.py:466
  74.5 1.2 %pad_maximum_fusion.6 = f32[3,8,2,2,768]{4,3,2,1,0:T(2,128)S(1)} fusion(f32[3,8,2,1,768]{4,3,2,1,0:T(1,128)} %collective-permute-done.5, f32[3,8,2,1,768]{4,3,2,1,0:T(1,128)S(1)} %get-tuple-element.30), kind=kLoop, calls=%fused_computation.10 | loop fusion | flops 73728 | bytes 589824 | tf_op jit(solution)/shard_map/concatenate | solution.py:425
  75.7 0.2 reshape.64.refs_5_
  75.9 1.1 %pad_maximum_fusion.5 = f32[3,8,2,2,768]{4,3,2,1,0:T(2,128)S(1)} fusion(f32[3,8,1,2,768]{4,3,2,1,0:T(2,128)} %collective-permute-done.4, f32[3,8,1,2,768]{4,3,2,1,0:T(2,128)S(1)} %get-tuple-element.32), kind=kLoop, calls=%fused_computation.9 | loop fusion | flops 73728 | bytes 589824 | tf_op jit(solution)/shard_map/concatenate | solution.py:425
  77.0 0.2 reshape.62.refs_4_
  77.3 6.1 %force.1 = (f32[4,8,24,128]{3,2,1,0:T(8,128)S(1)}, f32[3,8,24,128]{3,2,1,0:T(8,128)S(1)}, f32[3,8,24,128]{3,2,1,0:T(8,128)S(1)}) custom-call(f32[4,6]{1,0:T(4,128)S(1)} %copy-done.9, f32[4,12,24,128]{3,2,1,0:T(8,128)S(1)} %reshape.53.refs_0_.refs_1_, f32[6,18,24,128]{3,2,1,0:T(8,128)S(1)} %get-tuple-element.15.refs_2_, ...), custom_call_target="tpu_custom_call" | custom-call | tf_op jit(solution)/shard_map/force/pallas_call | solution.py:470
  83.4 0.7 copy-done.6
  84.1 0.7 copy-done.8
  84.8 1.2 %reshape.66 = f32[3,8,2,2,768]{4,3,2,1,0:T(2,128)S(1)} reshape(f32[3,8,24,128]{3,2,1,0:T(8,128)} %copy-done.8) | data formatting | bytes 589824 | tf_op jit(solution)/shard_map/reshape | solution.py:437
  86.3 0.2 fusion.12
  86.5 0.9 collective-permute-start.7
  87.4 0.6 broadcast_multiply_fusion
  88.0 0.2 reshape.65
  88.2 2.4 %collective-permute-done.6 = f32[3,8,1,2,768]{4,3,2,1,0:T(2,128)S(1)} collective-permute-done((f32[3,8,1,2,768]{4,3,2,1,0:T(2,128)S(1)}, f32[3,8,1,2,768]{4,3,2,1,0:T(2,128)S(1)}, u32[]{:S(2)}, u32[]{:S(2)}) %collective-permute-start.6) | collective-permute-done | bytes 147488 | tf_op jit(solution)/shard_map/ppermute | solution.py:433
  90.6 4.3 %collective-permute-done.7 = f32[3,8,2,1,768]{4,3,2,1,0:T(1,128)S(1)} collective-permute-done((f32[3,8,2,1,768]{4,3,2,1,0:T(1,128)S(1)}, f32[3,8,2,1,768]{4,3,2,1,0:T(1,128)S(1)}, u32[]{:S(2)}, u32[]{:S(2)}) %collective-permute-start.7) | collective-permute-done | bytes 147488 | tf_op jit(solution)/shard_map/ppermute | solution.py:433
  94.9 0.4 fusion
  95.7 0.7 copy-done.11
  (42 shorter events, 1.4 us)
Async XLA Ops:
  0.6 8.8 %copy-start.10 = (f32[4,2,2,3,2,2,768]{6,5,4,3,2,1,0:T(2,128)S(1)}, f32[4,2,2,3,2,2,768]{6,5,4,3,2,1,0:T(2,128)}, u32[]{:S(2)}) copy-start(f32[4,2,2,3,2,2,768]{6,5,4,3,2,1,0:T(2,128)} %param.3) | copy-start | bytes 1769476
  1.8 8.1 %collective-permute-start = (f32[3,2,2,3,1,2,768]{6,5,4,3,2,1,0:T(2,128)S(1)}, f32[3,2,2,3,1,2,768]{6,5,4,3,2,1,0:T(2,128)S(1)}, u32[]{:S(2)}, u32[]{:S(2)}) collective-permute-start(f32[3,2,2,3,1,2,768]{6,5,4,3,2,1,0:T(2,128)S(1)} %get-tuple-element.23), channel_id=1, source_target_pairs={{4,0},{8,4},{12,8},{0,12},{5,1},{9,5},{13,9},{1,13},{6,2},{10,6},{... | collective-permute-start | bytes 663560 | tf_op jit(solution)/shard_map/ppermute | solution.py:424
  5.8 8.1 %collective-permute-start.1 = (f32[3,2,2,3,2,1,768]{6,5,4,3,2,1,0:T(1,128)S(1)}, f32[3,2,2,3,2,1,768]{6,5,4,3,2,1,0:T(1,128)S(1)}, u32[]{:S(2)}, u32[]{:S(2)}) collective-permute-start(f32[3,2,2,3,2,1,768]{6,5,4,3,2,1,0:T(1,128)S(1)} %get-tuple-element.21), channel_id=1, source_target_pairs={{1,0},{2,1},{3,2},{0,3},{5,4},{6,5},{7,6},{4,7},{9,8},{10,9},{11,1... | collective-permute-start | bytes 663560 | tf_op jit(solution)/shard_map/ppermute | solution.py:424
  20.1 0.9 copy-start.4
  21.0 0.8 copy-start
  22.9 7.7 %collective-permute-start.3 = (f32[3,8,2,1,768]{4,3,2,1,0:T(1,128)}, f32[3,8,2,1,768]{4,3,2,1,0:T(1,128)}, u32[]{:S(2)}, u32[]{:S(2)}) collective-permute-start(f32[3,8,2,1,768]{4,3,2,1,0:T(1,128)} %get-tuple-element.34), channel_id=1, source_target_pairs={{0,1},{1,2},{2,3},{3,0},{4,5},{5,6},{6,7},{7,4},{8,9},{9,10},{10,1... | collective-permute-start | bytes 442376 | tf_op jit(solution)/shard_map/ppermute | solution.py:433
  24.3 8.4 %collective-permute-start.2 = (f32[3,8,1,2,768]{4,3,2,1,0:T(2,128)}, f32[3,8,1,2,768]{4,3,2,1,0:T(2,128)}, u32[]{:S(2)}, u32[]{:S(2)}) collective-permute-start(f32[3,8,1,2,768]{4,3,2,1,0:T(2,128)} %get-tuple-element.36), channel_id=1, source_target_pairs={{0,4},{4,8},{8,12},{12,0},{1,5},{5,9},{9,13},{13,1},{2,6},{6,10},{... | collective-permute-start | bytes 442376 | tf_op jit(solution)/shard_map/ppermute | solution.py:433
  25.6 9.2 %copy-start.9 = (f32[4,6]{1,0:T(4,128)S(1)}, f32[4,6]{1,0:T(4,128)}, u32[]{:S(2)}) copy-start(f32[4,6]{1,0:T(4,128)} %refs_0_.1) | copy-start | bytes 292
  34.8 1.1 %copy-start.1 = (f32[6,8,24,128]{3,2,1,0:T(8,128)S(1)}, f32[6,8,24,128]{3,2,1,0:T(8,128)}, u32[]{:S(2)}) copy-start(f32[6,8,24,128]{3,2,1,0:T(8,128)} %copy-done) | copy-start | bytes 1769476
  35.9 1.0 copy-start.2
  36.8 1.0 copy-start.3
  37.8 1.1 %copy-start.5 = (f32[6,8,24,128]{3,2,1,0:T(8,128)S(1)}, f32[6,8,24,128]{3,2,1,0:T(8,128)}, u32[]{:S(2)}) copy-start(f32[6,8,24,128]{3,2,1,0:T(8,128)} %copy-done.4) | copy-start | bytes 1769476
  40.3 34.2 %collective-permute-start.5 = (f32[3,8,2,1,768]{4,3,2,1,0:T(1,128)S(1)}, f32[3,8,2,1,768]{4,3,2,1,0:T(1,128)}, u32[]{:S(2)}, u32[]{:S(2)}) collective-permute-start(f32[3,8,2,1,768]{4,3,2,1,0:T(1,128)S(1)} %get-tuple-element.31), channel_id=1, source_target_pairs={{1,0},{2,1},{3,2},{0,3},{5,4},{6,5},{7,6},{4,7},{9,8},{10,9},{11,1... | collective-permute-start | bytes 442376 | tf_op jit(solution)/shard_map/ppermute | solution.py:424
  43.3 32.7 %collective-permute-start.4 = (f32[3,8,1,2,768]{4,3,2,1,0:T(2,128)}, f32[3,8,1,2,768]{4,3,2,1,0:T(2,128)}, u32[]{:S(2)}, u32[]{:S(2)}) collective-permute-start(f32[3,8,1,2,768]{4,3,2,1,0:T(2,128)} %get-tuple-element.33), channel_id=1, source_target_pairs={{4,0},{8,4},{12,8},{0,12},{5,1},{9,5},{13,9},{1,13},{6,2},{10,6},{... | collective-permute-start | bytes 442376 | tf_op jit(solution)/shard_map/ppermute | solution.py:424
  83.4 0.7 copy-start.6
  84.1 0.7 copy-start.8
  84.8 1.3 %copy-start.7 = (f32[3,8,24,128]{3,2,1,0:T(8,128)S(1)}, f32[3,8,24,128]{3,2,1,0:T(8,128)}, u32[]{:S(2)}) copy-start(f32[3,8,24,128]{3,2,1,0:T(8,128)} %copy-done.6) | copy-start | bytes 884740
  86.0 4.6 %collective-permute-start.6 = (f32[3,8,1,2,768]{4,3,2,1,0:T(2,128)S(1)}, f32[3,8,1,2,768]{4,3,2,1,0:T(2,128)S(1)}, u32[]{:S(2)}, u32[]{:S(2)}) collective-permute-start(f32[3,8,1,2,768]{4,3,2,1,0:T(2,128)S(1)} %get-tuple-element.26), channel_id=1, source_target_pairs={{0,4},{4,8},{8,12},{12,0},{1,5},{5,9},{9,13},{13,1},{2,6},{6,10},{... | collective-permute-start | bytes 442376 | tf_op jit(solution)/shard_map/ppermute | solution.py:433
  86.5 8.4 %collective-permute-start.7 = (f32[3,8,2,1,768]{4,3,2,1,0:T(1,128)S(1)}, f32[3,8,2,1,768]{4,3,2,1,0:T(1,128)S(1)}, u32[]{:S(2)}, u32[]{:S(2)}) collective-permute-start(f32[3,8,2,1,768]{4,3,2,1,0:T(1,128)S(1)} %get-tuple-element.28), channel_id=1, source_target_pairs={{0,1},{1,2},{2,3},{3,0},{4,5},{5,6},{6,7},{7,4},{8,9},{9,10},{10,1... | collective-permute-start | bytes 442376 | tf_op jit(solution)/shard_map/ppermute | solution.py:433
  95.7 0.7 copy-start.11
where the time goes:
time: 96.9 us; the launch traced here: 96.4 us
  blocking collectives  31 us (32%)
  local copies, waits for them, and re-layouts  20.6 us (21%)
  waiting for transfers between devices  15.1 us (16%)
  Pallas kernels  12.6 us (13%)
  starting transfers between devices  9.62 us (10%)
  other arithmetic  6.57 us (7%)
    psum x1, blocking collectives, body(): weight_grad = lax.psum(jnp.sum(sums, axis=1).reshape(4, 6), ('brick', 'tm'))  31 us
    ppermute x4, waiting for transfers between devices, behind(): last = lax.ppermute(last, axis, [(i, (i + 1) % n) for i in range(n)])  11.7 us
    ppermute x4, starting transfers between devices, ahead(): first = lax.ppermute(first, axis, [((i + 1) % n, i) for i in range(n)])  8.19 us
    unnamed x24, local copies, waits for them, and re-layouts  7.86 us
    pallas_call x1, Pallas kernels, body(): pl.pallas_call(lambda *refs: force_kernel(per_cell, *refs), out_shape=(si...  6.1 us
    pallas_call x1, Pallas kernels, body(): pl.pallas_call(lambda *refs: loops_kernel(per_cell, *refs), out_shape=(si...  5.47 us
    reshape x8, local copies, waits for them, and re-layouts, packed(): return values.reshape(-1, count, total, LANES)  4.87 us
    slice x4, local copies, waits for them, and re-layouts, ahead(): rest = lax.slice_in_dim(values, 1, values.shape[dim], axis=dim)  3.61 us
  transfers between devices with their start and end apart: 8, of which 4 were waited for; matrix products, arithmetic and copies ran while one was open for 11% of the time, Pallas kernels for 0%

commit v1 on v0

v1 whole, which is shorter than its diff:
```python
import jax
import jax.numpy as jnp
from jax import lax
from jax.experimental import pallas as pl
from jax.experimental.pallas import tpu as pltpu
from jax.sharding import PartitionSpec as P

NZ = 16
LANES = 128
ROOT_THREE = 3.0**0.5
VMEM = pl.BlockSpec(memory_space=pltpu.VMEM)
SMEM = pl.BlockSpec(memory_space=pltpu.SMEM)


def mul(a, b):
    return a[0] * b[0] - a[1] * b[1], a[0] * b[1] + a[1] * b[0]


def mul_conj(a, b):
    return a[0] * b[0] + a[1] * b[1], a[1] * b[0] - a[0] * b[1]


def add(*terms):
    re, im = terms[0]
    for t in terms[1:]:
        re, im = re + t[0], im + t[1]
    return re, im


def sub(a, b):
    return a[0] - b[0], a[1] - b[1]


def conj(a):
    return a[0], -a[1]


def scale(a, s):
    return a[0] * s, a[1] * s


def cross_row(r, s):
    out = []
    for i, j in ((1, 2), (2, 0), (0, 1)):
        out.append(conj(sub(mul(r[i], s[j]), mul(r[j], s[i]))))
    return out


def product(a, b):
    rows = [
        [add(mul(a[i][0], b[0][k]), mul(a[i][1], b[1][k]), mul(a[i][2], b[2][k])) for k in range(3)]
        for i in range(2)
    ]
    return rows + [cross_row(*rows)]


def product_dagger(a, b):
    rows = [
        [
            add(mul_conj(a[i][0], b[k][0]), mul_conj(a[i][1], b[k][1]), mul_conj(a[i][2], b[k][2]))
            for k in range(3)
        ]
        for i in range(2)
    ]
    return rows + [cross_row(*rows)]


def dagger(a):
    return [[conj(a[j][i]) for j in range(3)] for i in range(3)]


def conjugated(u, h):
    d0, d1, h01, h02, h12 = h
    t = []
    for i in range(2):
        a, b, c = u[i]
        t.append(
            [
                add(scale(a, d0), mul_conj(b, h01), mul_conj(c, h02)),
                add(scale(b, d1), mul(a, h01), mul_conj(c, h12)),
                add(mul(a, h02), mul(b, h12)),
            ]
        )

    def entry(i, j):
        return add(*[mul_conj(t[i][k], u[j][k]) for k in range(3)])

    def diagonal(i):
        return sum(t[i][k][0] * u[i][k][0] + t[i][k][1] * u[i][k][1] for k in range(3))

    e0, e1 = diagonal(0), diagonal(1)
    e2 = d0 + d1 - e0 - e1
    return e0 - e2, e1 - e2, entry(0, 1), entry(0, 2), entry(1, 2)


def flat(h):
    d0, d1, a, b, c = h
    return [d0, d1, *a, *b, *c]


def unflat(v):
    return v[0], v[1], (v[2], v[3]), (v[4], v[5]), (v[6], v[7])


def hermitian_part(p):
    return (
        [p[k][k][0] for k in range(3)],
        *[
            (0.5 * (p[i][j][0] + p[j][i][0]), 0.5 * (p[i][j][1] - p[j][i][1]))
            for i, j in ((0, 1), (0, 2), (1, 2))
        ],
    )


def anti_part(p):
    d = [p[k][k][1] for k in range(3)]
    return (
        d[0] - d[2],
        d[1] - d[2],
        *[
            (0.5 * (p[i][j][1] + p[j][i][1]), 0.5 * (p[j][i][0] - p[i][j][0]))
            for i, j in ((0, 1), (0, 2), (1, 2))
        ],
    )


def half_anticommutator(pr, q):
    p, p01, p02, p12 = pr
    d0, d1, q01, q02, q12 = q
    mean = (d0 + d1) * (1.0 / 3.0)
    q0, q1, q2 = d0 - mean, d1 - mean, -mean
    e01 = add(scale(q01, p[0] + p[1]), scale(p01, -q2), mul_conj(p02, q12), mul_conj(q02, p12))
    e02 = add(scale(q02, p[0] + p[2]), scale(p02, -q1), mul(p01, q12), mul(q01, p12))
    e12 = add(scale(q12, p[1] + p[2]), scale(p12, -q0), mul_conj(q02, p01), mul_conj(p02, q01))
    x01 = p01[0] * q01[0] + p01[1] * q01[1]
    x02 = p02[0] * q02[0] + p02[1] * q02[1]
    x12 = p12[0] * q12[0] + p12[1] * q12[1]
    last = p[2] * q2
    return (
        p[0] * q0 - last + x01 - x12,
        p[1] * q1 - last + x01 - x02,
        scale(e01, 0.5),
        scale(e02, 0.5),
        scale(e12, 0.5),
    )


def i_commutator(x, y):
    x0, x1, x01, x02, x12 = x
    y0, y1, y01, y02, y12 = y
    c01 = sub(add(scale(y01, x0 - x1), scale(x01, y1 - y0), mul_conj(x02, y12)), mul_conj(y02, x12))
    c02 = sub(add(scale(y02, x0), scale(x02, -y0), mul(x01, y12)), mul(y01, x12))
    c12 = sub(add(scale(y12, x1), scale(x12, -y1), mul_conj(y02, x01)), mul_conj(x02, y01))
    a01 = x01[1] * y01[0] - x01[0] * y01[1]
    a02 = x02[1] * y02[0] - x02[0] * y02[1]
    a12 = x12[1] * y12[0] - x12[0] * y12[1]
    d2 = 2.0 * (a02 + a12)
    return (
        -2.0 * (a01 + a02) - d2,
        2.0 * (a01 - a12) - d2,
        (-c01[1], c01[0]),
        (-c02[1], c02[0]),
        (-c12[1], c12[0]),
    )


def plane(p):
    mu = jnp.where(p < 3, 0, jnp.where(p < 5, 1, 2))
    nu = jnp.where(p < 3, p + 1, jnp.where(p < 5, p - 1, 3))
    return mu, nu


PLANES = ((0, 1), (0, 2), (0, 3), (1, 2), (1, 3), (2, 3))


def grid_of(shape):
    lane = lax.broadcasted_iota(jnp.int32, shape, 1)
    row = lax.broadcasted_iota(jnp.int32, shape, 0)
    return row, lane


def move_z(v, step):
    row, lane = grid_of(v.shape)
    inside = pltpu.roll(v, (-step) % LANES, 1)
    across = pltpu.roll(v, (step * (NZ - 1)) % LANES, 1)
    edge = NZ - 1 if step > 0 else 0
    return jnp.where(lane % NZ == edge, across, inside)


def move_y(v, step, per_cell):
    rows = v.shape[0]
    row, lane = grid_of(v.shape)
    turned = pltpu.roll(v, (-step * NZ) % LANES, 1)
    inside = pltpu.roll(turned, (-step) % rows, 0)
    across = pltpu.roll(turned, (step * (per_cell - 1)) % rows, 0)
    edge = per_cell - 1 if step > 0 else 0
    other = jnp.where(row % per_cell == edge, across, inside)
    over = lane >= LANES - NZ if step > 0 else lane < NZ
    return jnp.where(over, other, turned)


def load_matrix(ref, index, rows):
    at = lambda c: ref[(*index, c, rows, slice(None))]
    return [[(at(3 * i + j), at(9 + 3 * i + j)) for j in range(3)] for i in range(3)]


def store_matrix(ref, index, rows, m):
    for i in range(3):
        for j in range(3):
            for part in range(2):
                ref[(*index, 9 * part + 3 * i + j, rows, slice(None))] = m[i][j][part]


def load_flat(ref, index, rows):
    return unflat([ref[(*index, c, rows, slice(None))] for c in range(8)])


def store_flat(ref, index, rows, h):
    for c, v in enumerate(flat(h)):
        ref[(*index, c, rows, slice(None))] = v


def add_flat(ref, index, rows, h):
    for c, v in enumerate(flat(h)):
        ref[(*index, c, rows, slice(None))] += v

MESH = pl.DeviceIdType.MESH


class Side:
    def __init__(self, shift, period, shape):
        row, _ = grid_of(shape)
        self.rows = shape[0]
        self.shift = shift
        self.first = row % period < shift

    def turn(self, v, amount):
        return pltpu.roll(v, amount % self.rows, 0)

    def pack_first(self, v0, v1):
        return jnp.where(self.first, v0, self.turn(v1, self.shift))

    def pack_last(self, v0, v1):
        return jnp.where(self.first, self.turn(v0, -self.shift), v1)

    def ahead(self, v0, v1, got):
        s = self.shift
        return (
            jnp.where(self.first, self.turn(v0, -s), self.turn(got, s)),
            jnp.where(self.first, self.turn(v1, -s), got),
        )

    def behind(self, v0, v1, got):
        s = self.shift
        return (
            jnp.where(self.first, got, self.turn(v0, s)),
            jnp.where(self.first, self.turn(got, -s), self.turn(v1, s)),
        )


def chunk_loop(count, fn):
    def step(k, carry):
        fn(pl.ds(pl.multiple_of(8 * k, 8), 8))
        return carry

    lax.fori_loop(0, count, step, 0)


def index_loop(count, fn):
    def step(k, carry):
        fn(k)
        return carry

    lax.fori_loop(0, count, step, 0)


def third_row(full, index, chunks):
    def fn(rows):
        m = [
            [(full[(*index, 3 * i + j, rows, slice(None))], full[(*index, 9 + 3 * i + j, rows, slice(None))]) for j in range(3)]
            for i in range(2)
        ]
        for j, v in enumerate(cross_row(*m)):
            full[(*index, 6 + j, rows, slice(None))] = v[0]
            full[(*index, 15 + j, rows, slice(None))] = v[1]

    chunk_loop(chunks, fn)


X_PLANES = (0, 1, 2)
T_PLANES = (2, 4, 5)


def fused_kernel(
    nx, nt, per_cell, bricks, tms,
    weights, own, target,
    force_out, sums_out,
    full, plaq, here, moved_b, moved_c, res, force,
    link_x, link_x_in, link_t, link_t_in,
    vel_x, vel_x_in, vel_t, vel_t_in,
    res_x, res_x_in, res_t, res_t_in,
    for_x, for_x_in, for_t, for_t_in,
    sums_a, sums_b,
    sent, arrived, sent_a, arrived_a, sent_b, arrived_b,
):
    total = own.shape[2]
    chunks = total // 8
    g, bx, tm = lax.axis_index("groups"), lax.axis_index("brick"), lax.axis_index("tm")
    shape = (total, LANES)
    side_x = Side(nt * per_cell, nx * nt * per_cell, shape)
    side_t = Side(per_cell, nt * per_cell, shape)

    barrier = pltpu.get_barrier_semaphore()
    for k in range(1, bricks):
        pl.semaphore_signal(barrier, inc=1, device_id=(g, lax.rem(bx + k, bricks), tm), device_id_type=MESH)
    for k in range(1, tms):
        pl.semaphore_signal(barrier, inc=1, device_id=(g, bx, lax.rem(tm + k, tms)), device_id_type=MESH)

    x_ahead = (g, lax.rem(bx + 1, bricks), tm)
    x_behind = (g, lax.rem(bx + bricks - 1, bricks), tm)
    t_ahead = (g, bx, lax.rem(tm + 1, tms))
    t_behind = (g, bx, lax.rem(tm + tms - 1, tms))
    copies = []

    def send(src, dst, device):
        n = len(copies)
        copy = pltpu.make_async_remote_copy(
            src_ref=src, dst_ref=dst, send_sem=sent.at[n], recv_sem=arrived.at[n],
            device_id=device, device_id_type=MESH,
        )
        copy.start()
        copies.append(copy)
        return copy

    def pack_links(side, out, base):
        def fn(c):
            for k in range(3):
                out[k, c] = side.pack_first(own[base + k, 2 * c], own[base + k, 2 * c + 1])
        index_loop(6, fn)

    pack_links(side_t, link_t, 0)
    pack_links(side_x, link_x, 1)
    pl.semaphore_wait(barrier, bricks + tms - 2)
    got_link_t = send(link_t, link_t_in, t_behind)
    got_link_x = send(link_x, link_x_in, x_behind)

    for half in range(2):
        def copy_own(c):
            for d in range(4):
                full[0, d, c + 9 * half] = own[d, c + 6 * half]
        index_loop(6, copy_own)
    index_loop(4, lambda d: third_row(full, (0, d), chunks))

    def shift_links(c):
        for d in range(4):
            value = full[0, d, c]
            if d != 1:
                full[2, d, c] = move_y(value, 1, per_cell)
            if d != 2:
                full[3, d, c] = move_z(value, 1)

    index_loop(18, shift_links)

    def loop_plane(p):
        mu, nu = plane(p)

        def fn(rows):
            a = load_matrix(full, (0, mu), rows)
            b = load_matrix(full, (1 + mu, nu), rows)
            c = load_matrix(full, (1 + nu, mu), rows)
            d = load_matrix(full, (0, nu), rows)
            loop = product_dagger(product(a, b), product(d, c))
            store_matrix(plaq, (p,), rows, loop)
            pi = anti_part(loop)
            store_flat(here, (p,), rows, pi)
            store_flat(moved_b, (p,), rows, conjugated(dagger(a), pi))
            store_flat(moved_c, (p,), rows, conjugated(dagger(d), pi))

        chunk_loop(chunks, fn)

    def unpack_links(side, got, base, slot):
        for half in range(2):
            def fn(c):
                for k in range(3):
                    d = base + k
                    n = 2 * c + 9 * half
                    v = side.ahead(full[0, d, n], full[0, d, n + 1], got[k, c + 3 * half])
                    full[slot, d, n], full[slot, d, n + 1] = v
            index_loop(3, fn)
        index_loop(3, lambda k: third_row(full, (slot, base + k), chunks))

    def pack_flat(side, src, p, out, k):
        def fn(c):
            out[k, c] = side.pack_last(src[p, 2 * c], src[p, 2 * c + 1])
        index_loop(4, fn)

    loop_plane(3)
    got_link_x.wait_recv()
    unpack_links(side_x, link_x_in, 1, 1)
    index_loop(2, loop_plane)
    pack_flat(side_x, moved_b, 0, vel_x, 0)
    pack_flat(side_x, moved_b, 1, vel_x, 1)
    got_vel = [send(vel_x.at[k], vel_x_in.at[k], x_ahead) for k in range(2)]
    got_link_t.wait_recv()
    unpack_links(side_t, link_t_in, 0, 4)
    for k, p in enumerate(T_PLANES):
        loop_plane(p)
        pack_flat(side_t, moved_c, p, vel_t, k)
        got_vel.append(send(vel_t.at[k], vel_t_in.at[k], t_ahead))
        if p == 2:
            pack_flat(side_x, moved_b, 2, vel_x, 2)
            got_vel.append(send(vel_x.at[2], vel_x_in.at[2], x_ahead))

    def shift_back(c):
        for p in (3, 4):
            moved_b[p, c] = move_y(moved_b[p, c], -1, per_cell)
        moved_b[5, c] = move_z(moved_b[5, c], -1)
        moved_c[0, c] = move_y(moved_c[0, c], -1, per_cell)
        for p in (1, 3):
            moved_c[p, c] = move_z(moved_c[p, c], -1)

    index_loop(8, shift_back)
    for copy in got_vel:
        copy.wait_recv()

    def unpack_vel(c):
        for k in range(3):
            for side, dst, p, got in ((side_x, moved_b, X_PLANES[k], vel_x_in), (side_t, moved_c, T_PLANES[k], vel_t_in)):
                v = side.behind(dst[p, 2 * c], dst[p, 2 * c + 1], got[k, c])
                dst[p, 2 * c], dst[p, 2 * c + 1] = v

    index_loop(4, unpack_vel)

    def residual_chunk(k, carry):
        rows = pl.ds(pl.multiple_of(8 * k, 8), 8)
        acc = []
        load = lambda ref, index: [ref[index, c, rows, :] for c in range(8)]
        for mu in range(4):
            terms = []
            for nu in range(4):
                if nu == mu:
                    continue
                p = PLANES.index((min(mu, nu), max(mu, nu)))
                sign = 1.0 if mu < nu else -1.0
                terms.append((sign, load(here, p)))
                terms.append((-sign, load(moved_c if mu < nu else moved_b, p)))
            factors = [terms[s][0] * weights[mu, s] for s in range(6)]
            v = [sum(terms[s][1][c] * factors[s] for s in range(6)) for c in range(8)]
            t = [target[mu, a, rows, :] for a in range(8)]
            r3 = v[0] - v[1] - t[2]
            r8 = (v[0] + v[1]) * (1.0 / ROOT_THREE) - t[7]
            r = [
                r3 + ROOT_THREE * r8,
                ROOT_THREE * r8 - r3,
                2.0 * v[2] - t[0],
                2.0 * v[3] + t[1],
                2.0 * v[4] - t[3],
                2.0 * v[5] + t[4],
                2.0 * v[6] - t[5],
                2.0 * v[7] + t[6],
            ]
            for c in range(8):
                res[0, mu, c, rows, :] = r[c]
            part = r8 * (1.0 / ROOT_THREE)
            w = [r3 + part, part - r3] + [2.0 * x for x in r[2:]]
            for sign, term in terms:
                acc.append(sign * sum(w[c] * term[c] for c in range(8)))
        return tuple(x + y for x, y in zip(carry, acc))

    zero = jnp.zeros((8, LANES), jnp.float32)
    acc = lax.fori_loop(0, chunks, residual_chunk, (zero,) * 24)

    def pack_res(side, out, base):
        def fn(c):
            for k in range(3):
                out[k, c] = side.pack_first(res[0, base + k, 2 * c], res[0, base + k, 2 * c + 1])
        index_loop(4, fn)

    pack_res(side_t, res_t, 0)
    got_res_t = send(res_t, res_t_in, t_behind)
    pack_res(side_x, res_x, 1)
    got_res_x = send(res_x, res_x_in, x_behind)

    def share(values, count, me, device_of, sources, sends, arrivals):
        sources[me] = values
        out = []
        for k in range(1, count):
            copy = pltpu.make_async_remote_copy(
                src_ref=sources.at[me], dst_ref=sources.at[me],
                send_sem=sends.at[k - 1], recv_sem=arrivals.at[k - 1],
                device_id=device_of(lax.rem(me + k, count)), device_id_type=MESH,
            )
            copy.start()
            out.append(copy)
        return out

    local = jnp.concatenate([jnp.sum(x, axis=0, keepdims=True) for x in acc], axis=0)
    a_copies = share(local, tms, tm, lambda n: (g, bx, n), sums_a, sent_a, arrived_a)

    def shift_residual(c):
        for d in range(4):
            value = res[0, d, c]
            if d != 1:
                res[2, d, c] = move_y(value, 1, per_cell)
            if d != 2:
                res[3, d, c] = move_z(value, 1)
            force[d, c] = jnp.zeros_like(value)

    index_loop(8, shift_residual)

    def force_plane(p):
        mu, nu = plane(p)
        wa, wc = weights[mu, 2 * (nu - 1)], weights[mu, 2 * (nu - 1) + 1]
        wd, wb = weights[nu, 2 * mu], weights[nu, 2 * mu + 1]

        def fn(rows):
            a = load_matrix(full, (0, mu), rows)
            d = load_matrix(full, (0, nu), rows)
            loop = load_matrix(plaq, (p,), rows)
            pr, pi = hermitian_part(loop), anti_part(loop)
            sb = [x * wb for x in flat(conjugated(a, load_flat(res, (1 + mu, nu), rows)))]
            sc = [x * wc for x in flat(conjugated(d, load_flat(res, (1 + nu, mu), rows)))]
            ra = flat(load_flat(res, (0, mu), rows))
            rd = flat(load_flat(res, (0, nu), rows))
            q = unflat([wa * ra[c] - wd * rd[c] + sb[c] - sc[c] for c in range(8)])
            e = flat(half_anticommutator(pr, q))
            k = [0.5 * x for x in flat(i_commutator(pi, q))]
            fore = [x + y for x, y in zip(e, k)]
            aft = [y - x for x, y in zip(e, k)]
            store_flat(moved_b, (p,), rows, conjugated(dagger(a), unflat(fore)))
            store_flat(moved_c, (p,), rows, conjugated(dagger(d), unflat(aft)))
            xb = flat(i_commutator(pi, unflat(sb)))
            xc = flat(i_commutator(pi, unflat(sc)))
            add_flat(force, (mu,), rows, unflat([x - y for x, y in zip(fore, xb)]))
            add_flat(force, (nu,), rows, unflat([x + y for x, y in zip(aft, xc)]))

        chunk_loop(chunks, fn)

    def unpack_res(side, got, base, slot):
        def fn(c):
            for k in range(3):
                d = base + k
                v = side.ahead(res[0, d, 2 * c], res[0, d, 2 * c + 1], got[k, c])
                res[slot, d, 2 * c], res[slot, d, 2 * c + 1] = v
        index_loop(4, fn)

    force_plane(3)
    for copy in a_copies:
        copy.wait_recv()
    local = sum(sums_a[n] for n in range(tms))
    b_copies = share(local, bricks, bx, lambda n: (g, n, tm), sums_b, sent_b, arrived_b)
    got_res_x.wait_recv()
    unpack_res(side_x, res_x_in, 1, 1)
    index_loop(2, force_plane)
    pack_flat(side_x, moved_b, 0, for_x, 0)
    pack_flat(side_x, moved_b, 1, for_x, 1)
    got_for = [send(for_x.at[k], for_x_in.at[k], x_ahead) for k in range(2)]
    got_res_t.wait_recv()
    unpack_res(side_t, res_t_in, 0, 4)
    for k, p in enumerate(T_PLANES):
        force_plane(p)
        pack_flat(side_t, moved_c, p, for_t, k)
        got_for.append(send(for_t.at[k], for_t_in.at[k], t_ahead))
        if p == 2:
            pack_flat(side_x, moved_b, 2, for_x, 2)
            got_for.append(send(for_x.at[2], for_x_in.at[2], x_ahead))

    def add_back(c):
        force[2, c] += move_y(moved_b[3, c], -1, per_cell)
        force[3, c] += move_y(moved_b[4, c], -1, per_cell) + move_z(moved_b[5, c], -1)
        force[0, c] += move_y(moved_c[0, c], -1, per_cell) + move_z(moved_c[1, c], -1)
        force[1, c] += move_z(moved_c[3, c], -1)

    index_loop(8, add_back)
    for copy in b_copies:
        copy.wait_recv()
    sums_out[...] = sum(sums_b[n] for n in range(bricks))
    for copy in got_for:
        copy.wait_recv()

    def add_far(c):
        for k in range(3):
            for side, src, p, got, d in ((side_x, moved_b, X_PLANES[k], for_x_in, k + 1), (side_t, moved_c, T_PLANES[k], for_t_in, k)):
                v0, v1 = side.behind(src[p, 2 * c], src[p, 2 * c + 1], got[k, c])
                force[d, 2 * c] += v0
                force[d, 2 * c + 1] += v1

    index_loop(4, add_far)

    def write(rows):
        for d in range(4):
            h = [force[d, c, rows, :] for c in range(8)]
            out = [
                2.0 * h[2], -2.0 * h[3], h[0] - h[1], 2.0 * h[4], -2.0 * h[5],
                2.0 * h[6], -2.0 * h[7], (h[0] + h[1]) * (1.0 / ROOT_THREE),
            ]
            for a in range(8):
                force_out[d, a, rows, :] = out[a]

    chunk_loop(chunks, write)
    for copy in copies + a_copies + b_copies:
        copy.wait_send()


def body(link_rows, target, weights):
    f32 = jnp.float32
    nx, nt, plane_sites = link_rows.shape[4:]
    bricks, tms = lax.axis_size("brick"), lax.axis_size("tm")
    sites = nx * nt * plane_sites
    total = sites // LANES
    per_cell = plane_sites // LANES
    space = lambda *lead: pltpu.VMEM((*lead, total, LANES), f32)
    dma = pltpu.SemaphoreType.DMA
    force, sums = pl.pallas_call(
        lambda *refs: fused_kernel(nx, nt, per_cell, bricks, tms, *refs),
        out_shape=(
            jax.ShapeDtypeStruct((4, 8, total, LANES), f32),
            jax.ShapeDtypeStruct((24, LANES), f32),
        ),
        in_specs=[SMEM, VMEM, VMEM],
        out_specs=(VMEM, VMEM),
        scratch_shapes=[
            space(5, 4, 18), space(6, 18), space(6, 8), space(6, 8), space(6, 8),
            space(5, 4, 8), space(4, 8),
            *[space(3, 6)] * 4,
            *[space(3, 4)] * 12,
            pltpu.VMEM((tms, 24, LANES), f32), pltpu.VMEM((bricks, 24, LANES), f32),
            dma((16,)), dma((16,)), dma((tms,)), dma((tms,)), dma((bricks,)), dma((bricks,)),
        ],
        compiler_params=pltpu.CompilerParams(
            vmem_limit_bytes=48 * 1024 * 1024, collective_id=0, has_side_effects=True
        ),
        name="flow",
    )(
        weights,
        link_rows.reshape(4, 12, total, LANES),
        target.reshape(4, 8, total, LANES),
    )
    weight_grad = jnp.sum(sums, axis=1).reshape(4, 6) / (sites * bricks * tms)
    return weight_grad, force.reshape(4, 8, nx, nt, plane_sites)


def solution(mesh):
    in_specs = (
        P("groups", None, None, None, "brick", "tm", None),
        P("groups", None, "brick", "tm", None),
        P(),
    )
    out_specs = (P("groups", None), P("groups", None, "brick", "tm", None))
    return jax.shard_map(body, mesh=mesh, in_specs=in_specs, out_specs=out_specs, check_vma=False)
```

time: 96.9 us -> 36.8 us (0.38)
  blocking collectives: 31 us -> 0 us
  Pallas kernels: 12.6 us -> 32.2 us
  local copies, waits for them, and re-layouts: 20.6 us -> 3.67 us
  waiting for transfers between devices: 15.1 us -> 0 us
  starting transfers between devices: 9.62 us -> 0 us
  other arithmetic: 6.57 us -> 0.12 us
    psum x1 -> x0, blocking collectives: 31 us -> none  [body(): weight_grad = lax.psum(jnp.sum(sums, axis=1).reshape(4, 6), ('brick', 'tm'))]
    pallas_call x3 -> x1, Pallas kernels: 12.6 us -> 32.2 us  [body(): pl.pallas_call(lambda *refs: fused_kernel(nx, nt, per_cell, bricks, tms,...]
    ppermute x8 -> x0, waiting for transfers between devices: 15.1 us -> none  [the longest x4 11.7 us: behind(): last = lax.ppermute(last, axis, [(i, (i + 1) % n) for i in range(n)])]
    ppermute x8 -> x0, starting transfers between devices: 9.62 us -> none  [the longest x4 8.19 us: ahead(): first = lax.ppermute(first, axis, [((i + 1) % n, i) for i in range(n)])]
    unnamed x24 -> x4, local copies, waits for them, and re-layouts: 7.86 us -> 0.2 us
    slice x12 -> x0, local copies, waits for them, and re-layouts: 5.59 us -> none  [the longest x4 3.61 us: ahead(): rest = lax.slice_in_dim(values, 1, values.shape[dim], axis=dim)]
    concatenate x6 -> x0, other arithmetic: 5.15 us -> none  [the longest x4 2.84 us: ahead(): return jnp.concatenate([rest, first], axis=dim)]
    reshape x16 -> x3, local copies, waits for them, and re-layouts: 7.17 us -> 2.8 us  [the longest x1 1.37 us: body(): target.reshape(4, 8, total, LANES)]
  transfers between devices with their start and end apart: 8 -> 0, of which waited for: 4 -> 0; matrix products, arithmetic and copies ran while one was open for 11% -> 0% of each run, Pallas kernels for 0% -> 0%
where the time goes in v1:
time: 36.8 us; the launch traced here: 36.6 us
  Pallas kernels  32.2 us (88%)
  local copies, waits for them, and re-layouts  3.67 us (10%)
  between operations  0.67 us (2%)
    pallas_call x1, Pallas kernels, body(): pl.pallas_call(lambda *refs: fused_kernel(nx, nt, per_cell, bricks, tms,...  32.2 us
    reshape x1, local copies, waits for them, and re-layouts, body(): target.reshape(4, 8, total, LANES)  1.37 us
    reshape x1, local copies, waits for them, and re-layouts, body(): return (weight_grad, force.reshape(4, 8, nx, nt, plane_sites))  0.96 us

profile of v1, /device:TPU:0, one launch (start us, length us, event | category | flops | bytes accessed | tf_op | source)
XLA Modules:
  0.0 36.6 jit_solution(14271102672411579792)
XLA Ops:
  0.6 0.0 copy-start.1
  0.6 1.4 %reshape.17.refs_2_ = f32[4,8,24,128]{3,2,1,0:T(8,128)S(1)} reshape(f32[4,8,2,2,768]{4,3,2,1,0:T(2,128)} %param.4) | data formatting | bytes 786432 | tf_op jit(solution)/shard_map/reshape | solution.py:637
  2.0 0.0 copy-done.1
  2.0 0.0 copy-start
  2.0 0.5 %reshape.16.refs_1_ = f32[4,12,24,128]{3,2,1,0:T(8,128)S(1)} reshape(f32[4,2,2,3,2,2,768]{6,5,4,3,2,1,0:T(2,128)S(1)} %copy-done.1) | data formatting | bytes 1179648 | tf_op jit(solution)/shard_map/reshape | solution.py:636
  2.5 0.2 copy-done
  2.7 32.2 %flow.1 = (f32[4,8,24,128]{3,2,1,0:T(8,128)S(1)}, f32[24,128]{1,0:T(8,128)S(1)}) custom-call(f32[4,6]{1,0:T(4,128)S(1)} %copy-done, f32[4,12,24,128]{3,2,1,0:T(8,128)S(1)} %reshape.16.refs_1_, f32[4,8,24,128]{3,2,1,0:T(8,128)S(1)} %reshape.17.refs_2_), custom_call_target="tpu_custom_call" | custom-call | tf_op jit(solution)/shard_map/flow/pallas_call | solution.py:614
  34.9 0.1 reduce_sum.9
  35.0 0.7 %div.6 = f32[4,6]{1,0:T(4,128)} reshape(f32[24]{0:T(128)S(1)} %broadcast_multiply_fusion) | data formatting | bytes 192 | tf_op jit(solution)/shard_map/div | solution.py:639
  35.7 1.0 %reshape.18 = f32[4,8,2,2,768]{4,3,2,1,0:T(2,128)} reshape(f32[4,8,24,128]{3,2,1,0:T(8,128)S(1)} %get-tuple-element.5) | data formatting | bytes 786432 | tf_op jit(solution)/shard_map/reshape | solution.py:640
  (1 shorter events, 0.0 us)
Async XLA Ops:
  0.6 1.4 %copy-start.1 = (f32[4,2,2,3,2,2,768]{6,5,4,3,2,1,0:T(2,128)S(1)}, f32[4,2,2,3,2,2,768]{6,5,4,3,2,1,0:T(2,128)}, u32[]{:S(2)}) copy-start(f32[4,2,2,3,2,2,768]{6,5,4,3,2,1,0:T(2,128)} %param.3) | copy-start | bytes 1769476
  2.0 0.7 %copy-start = (f32[4,6]{1,0:T(4,128)S(1)}, f32[4,6]{1,0:T(4,128)}, u32[]{:S(2)}) copy-start(f32[4,6]{1,0:T(4,128)} %refs_0_.1) | copy-start | bytes 292

commit v2 on v1

--- a/solution.py
+++ b/solution.py
@@ -275,7 +275,8 @@
 
 
 def third_row(full, index, chunks):
-    def fn(rows):
+    for k in range(chunks):
+        rows = pl.ds(8 * k, 8)
         m = [
             [(full[(*index, 3 * i + j, rows, slice(None))], full[(*index, 9 + 3 * i + j, rows, slice(None))]) for j in range(3)]
             for i in range(2)
@@ -284,10 +285,7 @@
             full[(*index, 6 + j, rows, slice(None))] = v[0]
             full[(*index, 15 + j, rows, slice(None))] = v[1]
 
-    chunk_loop(chunks, fn)
-
-
-X_PLANES = (0, 1, 2)
+
 T_PLANES = (2, 4, 5)
 
 
@@ -332,17 +330,21 @@
         copies.append(copy)
         return copy
 
-    def pack_links(side, out, base):
-        def fn(c):
-            for k in range(3):
-                out[k, c] = side.pack_first(own[base + k, 2 * c], own[base + k, 2 * c + 1])
-        index_loop(6, fn)
-
-    pack_links(side_t, link_t, 0)
-    pack_links(side_x, link_x, 1)
+    def pack_links(side, out, base, k):
+        for c in range(6):
+            out[k, c] = side.pack_first(own[base + k, 2 * c], own[base + k, 2 * c + 1])
+
+    got_link_t, got_link_x = [None] * 3, [None] * 3
+    pack_links(side_t, link_t, 0, 0)
     pl.semaphore_wait(barrier, bricks + tms - 2)
-    got_link_t = send(link_t, link_t_in, t_behind)
-    got_link_x = send(link_x, link_x_in, x_behind)
+    got_link_t[0] = send(link_t.at[0], link_t_in.at[0], t_behind)
+    for out, k in (("x", 2), ("t", 1), ("x", 0), ("t", 2), ("x", 1)):
+        if out == "x":
+            pack_links(side_x, link_x, 1, k)
+            got_link_x[k] = send(link_x.at[k], link_x_in.at[k], x_behind)
+        else:
+            pack_links(side_t, link_t, 0, k)
+            got_link_t[k] = send(link_t.at[k], link_t_in.at[k], t_behind)
 
     for half in range(2):
         def copy_own(c):
@@ -378,38 +380,43 @@
 
         chunk_loop(chunks, fn)
 
-    def unpack_links(side, got, base, slot):
+    def unpack_links(side, copy, got, base, slot, k):
+        copy[k].wait_recv()
+        d = base + k
         for half in range(2):
-            def fn(c):
-                for k in range(3):
-                    d = base + k
-                    n = 2 * c + 9 * half
-                    v = side.ahead(full[0, d, n], full[0, d, n + 1], got[k, c + 3 * half])
-                    full[slot, d, n], full[slot, d, n + 1] = v
-            index_loop(3, fn)
-        index_loop(3, lambda k: third_row(full, (slot, base + k), chunks))
+            for c in range(3):
+                n = 2 * c + 9 * half
+                v = side.ahead(full[0, d, n], full[0, d, n + 1], got[k, c + 3 * half])
+                full[slot, d, n], full[slot, d, n + 1] = v
+        third_row(full, (slot, d), chunks)
 
     def pack_flat(side, src, p, out, k):
-        def fn(c):
+        for c in range(4):
             out[k, c] = side.pack_last(src[p, 2 * c], src[p, 2 * c + 1])
-        index_loop(4, fn)
+
+    got_vel_x, got_vel_t = [None] * 3, [None] * 3
+
+    def send_x(out, got, copy, k):
+        pack_flat(side_x, moved_b, k, out, k)
+        copy[k] = send(out.at[k], got.at[k], x_ahead)
+
+    def send_t(out, got, copy, k):
+        pack_flat(side_t, moved_c, T_PLANES[k], out, k)
+        copy[k] = send(out.at[k], got.at[k], t_ahead)
 
     loop_plane(3)
-    got_link_x.wait_recv()
-    unpack_links(side_x, link_x_in, 1, 1)
-    index_loop(2, loop_plane)
-    pack_flat(side_x, moved_b, 0, vel_x, 0)
-    pack_flat(side_x, moved_b, 1, vel_x, 1)
-    got_vel = [send(vel_x.at[k], vel_x_in.at[k], x_ahead) for k in range(2)]
-    got_link_t.wait_recv()
-    unpack_links(side_t, link_t_in, 0, 4)
-    for k, p in enumerate(T_PLANES):
-        loop_plane(p)
-        pack_flat(side_t, moved_c, p, vel_t, k)
-        got_vel.append(send(vel_t.at[k], vel_t_in.at[k], t_ahead))
-        if p == 2:
-            pack_flat(side_x, moved_b, 2, vel_x, 2)
-            got_vel.append(send(vel_x.at[2], vel_x_in.at[2], x_ahead))
+    for k in range(3):
+        if k == 0:
+            unpack_links(side_x, got_link_x, link_x_in, 1, 1, 2)
+        unpack_links(side_t, got_link_t, link_t_in, 0, 4, k)
+        loop_plane(T_PLANES[k])
+        send_t(vel_t, vel_t_in, got_vel_t, k)
+        if k == 0:
+            send_x(vel_x, vel_x_in, got_vel_x, 2)
+        if k < 2:
+            unpack_links(side_x, got_link_x, link_x_in, 1, 1, k)
+            loop_plane(k)
+            send_x(vel_x, vel_x_in, got_vel_x, k)
 
     def shift_back(c):
         for p in (3, 4):
@@ -420,22 +427,17 @@
             moved_c[p, c] = move_z(moved_c[p, c], -1)
 
     index_loop(8, shift_back)
-    for copy in got_vel:
-        copy.wait_recv()
-
-    def unpack_vel(c):
-        for k in range(3):
-            for side, dst, p, got in ((side_x, moved_b, X_PLANES[k], vel_x_in), (side_t, moved_c, T_PLANES[k], vel_t_in)):
-                v = side.behind(dst[p, 2 * c], dst[p, 2 * c + 1], got[k, c])
-                dst[p, 2 * c], dst[p, 2 * c + 1] = v
-
-    index_loop(4, unpack_vel)
-
-    def residual_chunk(k, carry):
-        rows = pl.ds(pl.multiple_of(8 * k, 8), 8)
-        acc = []
-        load = lambda ref, index: [ref[index, c, rows, :] for c in range(8)]
-        for mu in range(4):
+
+    def unpack_vel(side, copy, dst, p, got, k):
+        copy[k].wait_recv()
+        for c in range(4):
+            v = side.behind(dst[p, 2 * c], dst[p, 2 * c + 1], got[k, c])
+            dst[p, 2 * c], dst[p, 2 * c + 1] = v
+
+    def residual_of(mu):
+        def fn(k, carry):
+            rows = pl.ds(pl.multiple_of(8 * k, 8), 8)
+            load = lambda ref, index: [ref[index, c, rows, :] for c in range(8)]
             terms = []
             for nu in range(4):
                 if nu == mu:
@@ -463,23 +465,32 @@
                 res[0, mu, c, rows, :] = r[c]
             part = r8 * (1.0 / ROOT_THREE)
             w = [r3 + part, part - r3] + [2.0 * x for x in r[2:]]
-            for sign, term in terms:
-                acc.append(sign * sum(w[c] * term[c] for c in range(8)))
-        return tuple(x + y for x, y in zip(carry, acc))
-
-    zero = jnp.zeros((8, LANES), jnp.float32)
-    acc = lax.fori_loop(0, chunks, residual_chunk, (zero,) * 24)
-
-    def pack_res(side, out, base):
-        def fn(c):
-            for k in range(3):
-                out[k, c] = side.pack_first(res[0, base + k, 2 * c], res[0, base + k, 2 * c + 1])
-        index_loop(4, fn)
-
-    pack_res(side_t, res_t, 0)
-    got_res_t = send(res_t, res_t_in, t_behind)
-    pack_res(side_x, res_x, 1)
-    got_res_x = send(res_x, res_x_in, x_behind)
+            return tuple(
+                x + sign * sum(w[c] * term[c] for c in range(8)) for x, (sign, term) in zip(carry, terms)
+            )
+
+        zero = jnp.zeros((8, LANES), jnp.float32)
+        return lax.fori_loop(0, chunks, fn, (zero,) * 6)
+
+    def pack_res(side, out, base, k):
+        for c in range(4):
+            out[k, c] = side.pack_first(res[0, base + k, 2 * c], res[0, base + k, 2 * c + 1])
+
+    got_res_t, got_res_x = [None] * 3, [None] * 3
+    parts = [None] * 4
+    for mu in (0, 3, 1, 2):
+        if mu < 3:
+            unpack_vel(side_t, got_vel_t, moved_c, T_PLANES[mu], vel_t_in, mu)
+        if mu > 0:
+            unpack_vel(side_x, got_vel_x, moved_b, mu - 1, vel_x_in, mu - 1)
+        parts[mu] = residual_of(mu)
+        if mu < 3:
+            pack_res(side_t, res_t, 0, mu)
+            got_res_t[mu] = send(res_t.at[mu], res_t_in.at[mu], t_behind)
+        if mu > 0:
+            pack_res(side_x, res_x, 1, mu - 1)
+            got_res_x[mu - 1] = send(res_x.at[mu - 1], res_x_in.at[mu - 1], x_behind)
+    acc = [x for part in parts for x in part]
 
     def share(values, count, me, device_of, sources, sends, arrivals):
         sources[me] = values
@@ -536,34 +547,32 @@
 
         chunk_loop(chunks, fn)
 
-    def unpack_res(side, got, base, slot):
-        def fn(c):
-            for k in range(3):
-                d = base + k
-                v = side.ahead(res[0, d, 2 * c], res[0, d, 2 * c + 1], got[k, c])
-                res[slot, d, 2 * c], res[slot, d, 2 * c + 1] = v
-        index_loop(4, fn)
-
+    def unpack_res(side, copy, got, base, slot, k):
+        copy[k].wait_recv()
+        d = base + k
+        for c in range(4):
+            v = side.ahead(res[0, d, 2 * c], res[0, d, 2 * c + 1], got[k, c])
+            res[slot, d, 2 * c], res[slot, d, 2 * c + 1] = v
+
+    got_for_x, got_for_t = [None] * 3, [None] * 3
+    for k in range(3):
+        if k == 0:
+            unpack_res(side_x, got_res_x, res_x_in, 1, 1, 2)
+        unpack_res(side_t, got_res_t, res_t_in, 0, 4, k)
+        force_plane(T_PLANES[k])
+        send_t(for_t, for_t_in, got_for_t, k)
+        if k == 0:
+            send_x(for_x, for_x_in, got_for_x, 2)
+        if k < 2:
+            unpack_res(side_x, got_res_x, res_x_in, 1, 1, k)
+            force_plane(k)
+            send_x(for_x, for_x_in, got_for_x, k)
+        if k == 1:
+            for copy in a_copies:
+                copy.wait_recv()
+            local = sum(sums_a[n] for n in range(tms))
+            b_copies = share(local, bricks, bx, lambda n: (g, n, tm), sums_b, sent_b, arrived_b)
     force_plane(3)
-    for copy in a_copies:
-        copy.wait_recv()
-    local = sum(sums_a[n] for n in range(tms))
-    b_copies = share(local, bricks, bx, lambda n: (g, n, tm), sums_b, sent_b, arrived_b)
-    got_res_x.wait_recv()
-    unpack_res(side_x, res_x_in, 1, 1)
-    index_loop(2, force_plane)
-    pack_flat(side_x, moved_b, 0, for_x, 0)
-    pack_flat(side_x, moved_b, 1, for_x, 1)
-    got_for = [send(for_x.at[k], for_x_in.at[k], x_ahead) for k in range(2)]
-    got_res_t.wait_recv()
-    unpack_res(side_t, res_t_in, 0, 4)
-    for k, p in enumerate(T_PLANES):
-        force_plane(p)
-        pack_flat(side_t, moved_c, p, for_t, k)
-        got_for.append(send(for_t.at[k], for_t_in.at[k], t_ahead))
-        if p == 2:
-            pack_flat(side_x, moved_b, 2, for_x, 2)
-            got_for.append(send(for_x.at[2], for_x_in.at[2], x_ahead))
 
     def add_back(c):
         force[2, c] += move_y(moved_b[3, c], -1, per_cell)
@@ -575,17 +584,19 @@
     for copy in b_copies:
         copy.wait_recv()
     sums_out[...] = sum(sums_b[n] for n in range(bricks))
-    for copy in got_for:
-        copy.wait_recv()
-
-    def add_far(c):
-        for k in range(3):
-            for side, src, p, got, d in ((side_x, moved_b, X_PLANES[k], for_x_in, k + 1), (side_t, moved_c, T_PLANES[k], for_t_in, k)):
-                v0, v1 = side.behind(src[p, 2 * c], src[p, 2 * c + 1], got[k, c])
-                force[d, 2 * c] += v0
-                force[d, 2 * c + 1] += v1
-
-    index_loop(4, add_far)
+
+    def add_far(side, copy, src, p, got, d, k):
+        copy[k].wait_recv()
+        for c in range(4):
+            v0, v1 = side.behind(src[p, 2 * c], src[p, 2 * c + 1], got[k, c])
+            force[d, 2 * c] += v0
+            force[d, 2 * c + 1] += v1
+
+    add_far(side_x, got_for_x, moved_b, 2, for_x_in, 3, 2)
+    for k in range(3):
+        add_far(side_t, got_for_t, moved_c, T_PLANES[k], for_t_in, k, k)
+        if k < 2:
+            add_far(side_x, got_for_x, moved_b, k, for_x_in, k + 1, k)
 
     def write(rows):
         for d in range(4):
@@ -625,7 +636,7 @@
             *[space(3, 6)] * 4,
             *[space(3, 4)] * 12,
             pltpu.VMEM((tms, 24, LANES), f32), pltpu.VMEM((bricks, 24, LANES), f32),
-            dma((16,)), dma((16,)), dma((tms,)), dma((tms,)), dma((bricks,)), dma((bricks,)),
+            dma((24,)), dma((24,)), dma((tms,)), dma((tms,)), dma((bricks,)), dma((bricks,)),
         ],
         compiler_params=pltpu.CompilerParams(
             vmem_limit_bytes=48 * 1024 * 1024, collective_id=0, has_side_effects=True

time: 36.8 us -> 32.3 us (0.88)
  Pallas kernels: 32.2 us -> 27.6 us
    pallas_call x1, Pallas kernels: 32.2 us -> 27.6 us  [body(): pl.pallas_call(lambda *refs: fused_kernel(nx, nt, per_cell, bricks, tms,...]
where the time goes in v2:
time: 32.3 us; the launch traced here: 32.1 us
  Pallas kernels  27.6 us (85%)
  local copies, waits for them, and re-layouts  3.67 us (11%)
  between operations  0.67 us (2%)
    pallas_call x1, Pallas kernels, body(): pl.pallas_call(lambda *refs: fused_kernel(nx, nt, per_cell, bricks, tms,...  27.6 us
    reshape x1, local copies, waits for them, and re-layouts, body(): target.reshape(4, 8, total, LANES)  1.37 us
    reshape x1, local copies, waits for them, and re-layouts, body(): return (weight_grad, force.reshape(4, 8, nx, nt, plane_sites))  0.96 us
    div x1, local copies, waits for them, and re-layouts, body(): weight_grad = jnp.sum(sums, axis=1).reshape(4, 6) / (sites * bricks * tms)  0.67 us

profile of v2, /device:TPU:0, one launch (start us, length us, event | category | flops | bytes accessed | tf_op | source)
XLA Modules:
  0.0 32.1 jit_solution(7756576014921563985)
XLA Ops:
  0.6 0.0 copy-start.1
  0.6 1.4 %reshape.17.refs_2_ = f32[4,8,24,128]{3,2,1,0:T(8,128)S(1)} reshape(f32[4,8,2,2,768]{4,3,2,1,0:T(2,128)} %param.4) | data formatting | bytes 786432 | tf_op jit(solution)/shard_map/reshape | solution.py:648
  2.0 0.0 copy-done.1
  2.0 0.0 copy-start
  2.0 0.5 %reshape.16.refs_1_ = f32[4,12,24,128]{3,2,1,0:T(8,128)S(1)} reshape(f32[4,2,2,3,2,2,768]{6,5,4,3,2,1,0:T(2,128)S(1)} %copy-done.1) | data formatting | bytes 1179648 | tf_op jit(solution)/shard_map/reshape | solution.py:647
  2.5 0.2 copy-done
  2.7 27.6 %flow.1 = (f32[4,8,24,128]{3,2,1,0:T(8,128)S(1)}, f32[24,128]{1,0:T(8,128)S(1)}) custom-call(f32[4,6]{1,0:T(4,128)S(1)} %copy-done, f32[4,12,24,128]{3,2,1,0:T(8,128)S(1)} %reshape.16.refs_1_, f32[4,8,24,128]{3,2,1,0:T(8,128)S(1)} %reshape.17.refs_2_), custom_call_target="tpu_custom_call" | custom-call | tf_op jit(solution)/shard_map/flow/pallas_call | solution.py:625
  30.3 0.1 reduce_sum.9
  30.5 0.7 %div.6 = f32[4,6]{1,0:T(4,128)} reshape(f32[24]{0:T(128)S(1)} %broadcast_multiply_fusion) | data formatting | bytes 192 | tf_op jit(solution)/shard_map/div | solution.py:650
  31.1 1.0 %reshape.18 = f32[4,8,2,2,768]{4,3,2,1,0:T(2,128)} reshape(f32[4,8,24,128]{3,2,1,0:T(8,128)S(1)} %get-tuple-element.5) | data formatting | bytes 786432 | tf_op jit(solution)/shard_map/reshape | solution.py:651
  (1 shorter events, 0.0 us)
Async XLA Ops:
  0.6 1.4 %copy-start.1 = (f32[4,2,2,3,2,2,768]{6,5,4,3,2,1,0:T(2,128)S(1)}, f32[4,2,2,3,2,2,768]{6,5,4,3,2,1,0:T(2,128)}, u32[]{:S(2)}) copy-start(f32[4,2,2,3,2,2,768]{6,5,4,3,2,1,0:T(2,128)} %param.3) | copy-start | bytes 1769476
  2.0 0.7 %copy-start = (f32[4,6]{1,0:T(4,128)S(1)}, f32[4,6]{1,0:T(4,128)}, u32[]{:S(2)}) copy-start(f32[4,6]{1,0:T(4,128)} %refs_0_.1) | copy-start | bytes 292

commit v3 on v2

--- a/solution.py
+++ b/solution.py
@@ -338,7 +338,7 @@
     pack_links(side_t, link_t, 0, 0)
     pl.semaphore_wait(barrier, bricks + tms - 2)
     got_link_t[0] = send(link_t.at[0], link_t_in.at[0], t_behind)
-    for out, k in (("x", 2), ("t", 1), ("x", 0), ("t", 2), ("x", 1)):
+    for out, k in (("x", 0), ("t", 1), ("x", 2), ("t", 2), ("x", 1)):
         if out == "x":
             pack_links(side_x, link_x, 1, k)
             got_link_x[k] = send(link_x.at[k], link_x_in.at[k], x_behind)
@@ -404,8 +404,12 @@
         pack_flat(side_t, moved_c, T_PLANES[k], out, k)
         copy[k] = send(out.at[k], got.at[k], t_ahead)
 
-    loop_plane(3)
-    for k in range(3):
+    for side, k in (("x", 0), ("t", 0), ("x", 1), ("t", 1), ("t", 2)):
+        if side == "x":
+            unpack_links(side_x, got_link_x, link_x_in, 1, 1, k)
+            loop_plane(k)
+            send_x(vel_x, vel_x_in, got_vel_x, k)
+            continue
         if k == 0:
             unpack_links(side_x, got_link_x, link_x_in, 1, 1, 2)
         unpack_links(side_t, got_link_t, link_t_in, 0, 4, k)
@@ -413,10 +417,7 @@
         send_t(vel_t, vel_t_in, got_vel_t, k)
         if k == 0:
             send_x(vel_x, vel_x_in, got_vel_x, 2)
-        if k < 2:
-            unpack_links(side_x, got_link_x, link_x_in, 1, 1, k)
-            loop_plane(k)
-            send_x(vel_x, vel_x_in, got_vel_x, k)
+    loop_plane(3)
 
     def shift_back(c):
         for p in (3, 4):
@@ -563,15 +564,14 @@
         send_t(for_t, for_t_in, got_for_t, k)
         if k == 0:
             send_x(for_x, for_x_in, got_for_x, 2)
-        if k < 2:
-            unpack_res(side_x, got_res_x, res_x_in, 1, 1, k)
-            force_plane(k)
-            send_x(for_x, for_x_in, got_for_x, k)
-        if k == 1:
-            for copy in a_copies:
-                copy.wait_recv()
-            local = sum(sums_a[n] for n in range(tms))
-            b_copies = share(local, bricks, bx, lambda n: (g, n, tm), sums_b, sent_b, arrived_b)
+    for copy in a_copies:
+        copy.wait_recv()
+    local = sum(sums_a[n] for n in range(tms))
+    b_copies = share(local, bricks, bx, lambda n: (g, n, tm), sums_b, sent_b, arrived_b)
+    for k in range(2):
+        unpack_res(side_x, got_res_x, res_x_in, 1, 1, k)
+        force_plane(k)
+        send_x(for_x, for_x_in, got_for_x, k)
     force_plane(3)
 
     def add_back(c):
@@ -595,8 +595,8 @@
     add_far(side_x, got_for_x, moved_b, 2, for_x_in, 3, 2)
     for k in range(3):
         add_far(side_t, got_for_t, moved_c, T_PLANES[k], for_t_in, k, k)
-        if k < 2:
-            add_far(side_x, got_for_x, moved_b, k, for_x_in, k + 1, k)
+    for k in range(2):
+        add_far(side_x, got_for_x, moved_b, k, for_x_in, k + 1, k)
 
     def write(rows):
         for d in range(4):

time: 32.3 us -> 31.9 us (0.988)
  Pallas kernels: 27.6 us -> 27.2 us
    pallas_call x1, Pallas kernels: 27.6 us -> 27.2 us  [body(): pl.pallas_call(lambda *refs: fused_kernel(nx, nt, per_cell, bricks, tms,...]
where the time goes in v3:
time: 31.9 us; the launch traced here: 31.7 us
  Pallas kernels  27.2 us (85%)
  local copies, waits for them, and re-layouts  3.67 us (12%)
  between operations  0.67 us (2%)
    pallas_call x1, Pallas kernels, body(): pl.pallas_call(lambda *refs: fused_kernel(nx, nt, per_cell, bricks, tms,...  27.2 us
    reshape x1, local copies, waits for them, and re-layouts, body(): target.reshape(4, 8, total, LANES)  1.37 us
    reshape x1, local copies, waits for them, and re-layouts, body(): return (weight_grad, force.reshape(4, 8, nx, nt, plane_sites))  0.96 us
    div x1, local copies, waits for them, and re-layouts, body(): weight_grad = jnp.sum(sums, axis=1).reshape(4, 6) / (sites * bricks * tms)  0.67 us

profile of v3, /device:TPU:0, one launch (start us, length us, event | category | flops | bytes accessed | tf_op | source)
XLA Modules:
  0.0 31.7 jit_solution(13259151235488279019)
XLA Ops:
  0.6 0.0 copy-start.1
  0.6 1.4 %reshape.17.refs_2_ = f32[4,8,24,128]{3,2,1,0:T(8,128)S(1)} reshape(f32[4,8,2,2,768]{4,3,2,1,0:T(2,128)} %param.4) | data formatting | bytes 786432 | tf_op jit(solution)/shard_map/reshape | solution.py:648
  2.0 0.0 copy-done.1
  2.0 0.0 copy-start
  2.0 0.5 %reshape.16.refs_1_ = f32[4,12,24,128]{3,2,1,0:T(8,128)S(1)} reshape(f32[4,2,2,3,2,2,768]{6,5,4,3,2,1,0:T(2,128)S(1)} %copy-done.1) | data formatting | bytes 1179648 | tf_op jit(solution)/shard_map/reshape | solution.py:647
  2.5 0.2 copy-done
  2.7 27.2 %flow.1 = (f32[4,8,24,128]{3,2,1,0:T(8,128)S(1)}, f32[24,128]{1,0:T(8,128)S(1)}) custom-call(f32[4,6]{1,0:T(4,128)S(1)} %copy-done, f32[4,12,24,128]{3,2,1,0:T(8,128)S(1)} %reshape.16.refs_1_, f32[4,8,24,128]{3,2,1,0:T(8,128)S(1)} %reshape.17.refs_2_), custom_call_target="tpu_custom_call" | custom-call | tf_op jit(solution)/shard_map/flow/pallas_call | solution.py:625
  30.0 0.1 reduce_sum.9
  30.1 0.7 %div.6 = f32[4,6]{1,0:T(4,128)} reshape(f32[24]{0:T(128)S(1)} %broadcast_multiply_fusion) | data formatting | bytes 192 | tf_op jit(solution)/shard_map/div | solution.py:650
  30.8 1.0 %reshape.18 = f32[4,8,2,2,768]{4,3,2,1,0:T(2,128)} reshape(f32[4,8,24,128]{3,2,1,0:T(8,128)S(1)} %get-tuple-element.5) | data formatting | bytes 786432 | tf_op jit(solution)/shard_map/reshape | solution.py:651
  (1 shorter events, 0.0 us)
Async XLA Ops:
  0.6 1.4 %copy-start.1 = (f32[4,2,2,3,2,2,768]{6,5,4,3,2,1,0:T(2,128)S(1)}, f32[4,2,2,3,2,2,768]{6,5,4,3,2,1,0:T(2,128)}, u32[]{:S(2)}) copy-start(f32[4,2,2,3,2,2,768]{6,5,4,3,2,1,0:T(2,128)} %param.3) | copy-start | bytes 1769476
  2.0 0.7 %copy-start = (f32[4,6]{1,0:T(4,128)S(1)}, f32[4,6]{1,0:T(4,128)}, u32[]{:S(2)}) copy-start(f32[4,6]{1,0:T(4,128)} %refs_0_.1) | copy-start | bytes 292
